TPU v7x, 128 devices: a whole 4x4x4 slice. The times are simulated.
128 devices in a mesh: outer: 16 (over z_hi, x, core), inner: 8 (over y, z_lo).
Axes of the slice: x: 4, y: 4, z: 4 (z_hi: 2, z_lo: 2; z = z_hi * 2 + z_lo), core: 2. Of those that a mesh axis runs over, the one named last changes fastest.
Arguments:
- queries: bfloat16 [32768, 1024], P(('outer', 'inner')), may hold values from -8 to 8
- keys: bfloat16 [32768, 1024], P(('outer', 'inner')), may hold values from -8 to 8
- values: bfloat16 [32768, 1024], P(('outer', 'inner')), may hold values from -6 to 6
- d_output: bfloat16 [32768, 1024], P(('outer', 'inner')), may hold values from -6 to 6
Outputs:
- grad_queries: bfloat16 [32768, 1024], P(('outer', 'inner'))
- grad_keys: bfloat16 [32768, 1024], P(('outer', 'inner'))
- grad_values: bfloat16 [32768, 1024], P(('outer', 'inner'))
All inputs are finite; a program needn't handle non-finite values.
Results may differ from a plain program's by a relative error of at most 0.012.
The roundings to bfloat16 on the way count: a program that leaves them out, or rounds other values in their place, can miss the bound.
Values may be sent and summed in bfloat16 or wider, within the bound.
A program may use at most 128 MiB of HBM per device.

v0:
```python
import jax
import jax.numpy as jnp
from jax import lax
from jax.sharding import PartitionSpec as P

HEADS = 16


group_heads = 2


def shifted(block, axis, distance):
    devices = range(lax.axis_size(axis))
    route = [((i - distance) % len(devices), i) for i in devices]
    return lax.ppermute(block, axis, route)


def heads_of(array, start, width_cols):
    piece = array[:, start : start + width_cols]
    return piece.reshape(array.shape[0], group_heads, width_cols // group_heads)


def group_window(q_group, do_group, k_group, v_group, scale):
    score = jnp.einsum("thd,shd->hts", q_group, k_group, preferred_element_type=jnp.float32) * scale
    top = jnp.max(score, axis=-1, keepdims=True)
    lse = top + jnp.log(jnp.sum(jnp.exp(score - top), axis=-1, keepdims=True))
    prob = jnp.exp(score - lse)
    prob_low = prob.astype(jnp.bfloat16)
    output = jnp.einsum("hts,shd->thd", prob_low, v_group, preferred_element_type=jnp.float32)
    delta = jnp.transpose(jnp.sum(do_group.astype(jnp.float32) * output, axis=-1))
    dprob = jnp.einsum("thd,shd->hts", do_group, v_group, preferred_element_type=jnp.float32)
    dscore = (prob * (dprob - delta[:, :, None])).astype(jnp.bfloat16)
    grad_q = jnp.einsum("hts,shd->thd", dscore, k_group, preferred_element_type=jnp.float32) * scale
    grad_k = jnp.einsum("hts,thd->shd", dscore, q_group, preferred_element_type=jnp.float32) * scale
    grad_v = jnp.einsum("hts,thd->shd", prob_low, do_group, preferred_element_type=jnp.float32)
    return (grad_q, grad_k, grad_v, lse[:, :, 0], delta)


def local(queries, keys, values, d_output):
    rows = queries.shape[0]
    width = queries.shape[1]
    head_size = width // HEADS
    group_cols = group_heads * head_size
    scale = head_size ** (-0.5)
    paired = jnp.stack([keys, values])
    from_inner = shifted(paired, "inner", 1)
    from_outer = shifted(paired, "outer", 1)
    key_all = jnp.concatenate([keys, from_inner[0], from_outer[0]], axis=0)
    value_all = jnp.concatenate([values, from_inner[1], from_outer[1]], axis=0)
    keep = 3 * rows
    grad_q_parts, grad_k_parts, grad_v_parts, lse_parts, delta_parts = ([], [], [], [], [])
    for group in range(width // group_cols):
        start = group * group_cols
        grad_q, grad_k, grad_v, lse, delta = group_window(
            heads_of(queries, start, group_cols),
            heads_of(d_output, start, group_cols),
            heads_of(key_all, start, group_cols),
            heads_of(value_all, start, group_cols),
            scale,
        )
        grad_q_parts.append(grad_q.reshape(rows, group_cols))
        grad_k_parts.append(grad_k.reshape(keep, group_cols))
        grad_v_parts.append(grad_v.reshape(keep, group_cols))
        lse_parts.append(lse)
        delta_parts.append(delta)
    grad_queries = jnp.concatenate(grad_q_parts, axis=1)
    grad_k_all = jnp.concatenate(grad_k_parts, axis=1)
    grad_v_all = jnp.concatenate(grad_v_parts, axis=1)
    back_inner = shifted(
        jnp.stack([grad_k_all[rows : 2 * rows], grad_v_all[rows : 2 * rows]]).astype(jnp.bfloat16),
        "inner",
        -1,
    ).astype(jnp.float32)
    back_outer = shifted(
        jnp.stack([grad_k_all[2 * rows :], grad_v_all[2 * rows :]]).astype(jnp.bfloat16),
        "outer",
        -1,
    ).astype(jnp.float32)
    grad_keys = grad_k_all[:rows] + back_inner[0] + back_outer[0]
    grad_values = grad_v_all[:rows] + back_inner[1] + back_outer[1]
    return (
        grad_queries.astype(jnp.bfloat16),
        grad_keys.astype(jnp.bfloat16),
        grad_values.astype(jnp.bfloat16),
    )


def solution(mesh):
    in_specs = (
        P(("outer", "inner"), None),
        P(("outer", "inner"), None),
        P(("outer", "inner"), None),
        P(("outer", "inner"), None),
    )
    out_specs = (
        P(("outer", "inner"), None),
        P(("outer", "inner"), None),
        P(("outer", "inner"), None),
    )
    return jax.shard_map(local, mesh=mesh, in_specs=in_specs, out_specs=out_specs, check_vma=False)
```

profile of v0, /device:TPU:0, one launch (start us, length us, event | category | flops | bytes accessed | tf_op | source)
XLA Modules:
  0.0 143.6 jit_solution(12847858076440004694)
XLA Ops:
  0.6 1.4 pad_maximum_fusion.2
  2.1 2.1 %collective-permute-start = (bf16[2,256,1024]{2,1,0:T(8,128)(2,1)S(1)}, bf16[2,256,1024]{2,1,0:T(8,128)(2,1)}, u32[]{:S(2)}, u32[]{:S(2)}) collective-permute-start(bf16[2,256,1024]{2,1,0:T(8,128)(2,1)S(1)} %pad_maximum_fusion.2), channel_id=1, source_target_pairs={{7,0},{0,1},{1,2},{2,3},{3,4},{4,5},{5,6},{6,7},{15,8},{8,9},{9,10... | collective-permute-start | bytes 3145736 | tf_op jit(solution)/shard_map/ppermute | solution.py:15
  12.4 8.0 %collective-permute-done.1 = bf16[2,256,1024]{2,1,0:T(8,128)(2,1)} collective-permute-done((bf16[2,256,1024]{2,1,0:T(8,128)(2,1)S(1)}, bf16[2,256,1024]{2,1,0:T(8,128)(2,1)}, u32[]{:S(2)}, u32[]{:S(2)}) %collective-permute-start.1) | collective-permute-done | bytes 1048608 | tf_op jit(solution)/shard_map/ppermute | solution.py:15
  20.4 1.3 slice_bitcast_fusion.8
  21.7 19.5 %collective-permute-done = bf16[2,256,1024]{2,1,0:T(8,128)(2,1)} collective-permute-done((bf16[2,256,1024]{2,1,0:T(8,128)(2,1)S(1)}, bf16[2,256,1024]{2,1,0:T(8,128)(2,1)}, u32[]{:S(2)}, u32[]{:S(2)}) %collective-permute-start) | collective-permute-done | bytes 1048608 | tf_op jit(solution)/shard_map/ppermute | solution.py:15
  41.2 1.3 slice_bitcast_fusion.9
  43.0 1.1 fusion.95
  44.3 1.1 fusion.94
  45.4 1.1 copy.9
  55.4 0.9 fusion.50
  59.1 0.9 fusion.51
  59.9 1.1 convolution_multiply_fusion.12
  62.2 1.1 fusion.79
  64.3 0.9 fusion.52
  65.2 1.1 convolution_multiply_fusion.11
  67.4 1.3 fusion.76
  69.7 0.9 fusion.53
  70.6 1.2 convolution_multiply_fusion.10
  72.9 1.1 fusion.73
  75.8 1.1 convolution_multiply_fusion.9
  77.2 0.9 copy.71
  78.1 1.6 %copy.55 = bf16[256,128]{1,0:T(8,128)(2,1)} copy(bf16[256,128]{0,1:T(8,128)(2,1)} %bitcast.532) | data formatting | bytes 131072 | tf_op jit(solution)/shard_map/reshape | solution.py:61
  79.7 0.9 copy.87
  80.6 0.9 copy.72
  82.2 0.9 copy.88
  84.0 0.9 copy.89
  85.9 0.9 copy.90
  87.0 1.6 %copy.59 = bf16[256,128]{1,0:T(8,128)(2,1)} copy(bf16[256,128]{0,1:T(8,128)(2,1)} %bitcast.536) | data formatting | bytes 131072 | tf_op jit(solution)/shard_map/reshape | solution.py:61
  88.5 0.9 copy.91
  89.6 1.6 %copy.60 = bf16[256,128]{1,0:T(8,128)(2,1)} copy(bf16[256,128]{0,1:T(8,128)(2,1)} %bitcast.537) | data formatting | bytes 131072 | tf_op jit(solution)/shard_map/reshape | solution.py:61
  91.2 0.9 copy.92
  92.1 1.1 copy.77
  93.3 1.6 %copy.61 = bf16[256,128]{1,0:T(8,128)(2,1)} copy(bf16[256,128]{0,1:T(8,128)(2,1)} %bitcast.538) | data formatting | bytes 131072 | tf_op jit(solution)/shard_map/reshape | solution.py:61
  94.9 0.9 copy.93
  96.6 1.1 fusion.70
  99.0 1.2 convolution_multiply_fusion.8
  100.1 1.9 %copy.78 = f32[768,128]{1,0:T(8,128)} copy(f32[768,128]{0,1:T(8,128)} %bitcast.491) | data formatting | bytes 786432 | tf_op jit(solution)/shard_map/reshape | solution.py:62
  102.0 2.0 %copy.94 = f32[768,128]{1,0:T(8,128)} copy(f32[768,128]{0,1:T(8,128)} %bitcast.490) | data formatting | bytes 786432 | tf_op jit(solution)/shard_map/reshape | solution.py:63
  104.1 1.1 constant_dynamic-update-slice_fusion.22
  106.7 1.4 copy-done
  108.2 0.9 copy-done.6
  110.6 1.4 copy-done.1
  112.1 1.1 pad_maximum_fusion.4
  113.2 1.1 pad_maximum_fusion.3
  114.3 2.3 %collective-permute-start.2 = (bf16[2,256,1024]{2,1,0:T(8,128)(2,1)}, bf16[2,256,1024]{2,1,0:T(8,128)(2,1)S(1)}, u32[]{:S(2)}, u32[]{:S(2)}) collective-permute-start(bf16[2,256,1024]{2,1,0:T(8,128)(2,1)} %pad_maximum_fusion.3), channel_id=1, source_target_pairs={{1,0},{2,1},{3,2},{4,3},{5,4},{6,5},{7,6},{0,7},{9,8},{10,9},{11,1... | collective-permute-start | bytes 3145736 | tf_op jit(solution)/shard_map/ppermute | solution.py:15
  118.2 13.9 %collective-permute-done.3 = bf16[2,256,1024]{2,1,0:T(8,128)(2,1)S(1)} collective-permute-done((bf16[2,256,1024]{2,1,0:T(8,128)(2,1)}, bf16[2,256,1024]{2,1,0:T(8,128)(2,1)S(1)}, u32[]{:S(2)}, u32[]{:S(2)}) %collective-permute-start.3) | collective-permute-done | bytes 1048608 | tf_op jit(solution)/shard_map/ppermute | solution.py:15
  132.3 8.0 %collective-permute-done.2 = bf16[2,256,1024]{2,1,0:T(8,128)(2,1)S(1)} collective-permute-done((bf16[2,256,1024]{2,1,0:T(8,128)(2,1)}, bf16[2,256,1024]{2,1,0:T(8,128)(2,1)S(1)}, u32[]{:S(2)}, u32[]{:S(2)}) %collective-permute-start.2) | collective-permute-done | bytes 1048608 | tf_op jit(solution)/shard_map/ppermute | solution.py:15
  140.5 3.1 %fusion.65 = (bf16[256,1024]{1,0:T(8,128)(2,1)}, bf16[256,1024]{1,0:T(8,128)(2,1)}) fusion(f32[2,256,1024]{2,1,0:T(8,128)S(1)} %convert_element_type.112, f32[2,256,1024]{2,1,0:T(8,128)S(1)} %convert_element_type.111, f32[768,1024]{1,0:T(8,128)} %copy-done, f32[768,1024]{1,0:T(8,128)} %copy-done.1), kind=kLoop, calls=%fused_computation.132 | loop fusion | flops 1572864 | bytes 7340032 | tf_op jit(solution)/shard_map/convert_element_type | solution.py:84
  (227 shorter events, 37.3 us)
Async XLA Ops:
  0.6 3.5 %copy-start.41 = (bf16[256,1024]{1,0:T(8,128)(2,1)S(1)}, bf16[256,1024]{1,0:T(8,128)(2,1)}, u32[]{:S(2)}) copy-start(bf16[256,1024]{1,0:T(8,128)(2,1)} %param.4) | copy-start | bytes 1572868
  2.0 6.3 %copy-start.42 = (bf16[256,1024]{1,0:T(8,128)(2,1)S(1)}, bf16[256,1024]{1,0:T(8,128)(2,1)}, u32[]{:S(2)}) copy-start(bf16[256,1024]{1,0:T(8,128)(2,1)} %param.7) | copy-start | bytes 1572868
  2.0 18.4 %collective-permute-start.1 = (bf16[2,256,1024]{2,1,0:T(8,128)(2,1)S(1)}, bf16[2,256,1024]{2,1,0:T(8,128)(2,1)}, u32[]{:S(2)}, u32[]{:S(2)}) collective-permute-start(bf16[2,256,1024]{2,1,0:T(8,128)(2,1)S(1)} %pad_maximum_fusion.2), channel_id=1, source_target_pairs={{120,0},{0,8},{8,16},{16,24},{24,32},{32,40},{40,48},{48,56},{56,6... | collective-permute-start | bytes 3145736 | tf_op jit(solution)/shard_map/ppermute | solution.py:15
  2.1 39.1 %collective-permute-start = (bf16[2,256,1024]{2,1,0:T(8,128)(2,1)S(1)}, bf16[2,256,1024]{2,1,0:T(8,128)(2,1)}, u32[]{:S(2)}, u32[]{:S(2)}) collective-permute-start(bf16[2,256,1024]{2,1,0:T(8,128)(2,1)S(1)} %pad_maximum_fusion.2), channel_id=1, source_target_pairs={{7,0},{0,1},{1,2},{2,3},{3,4},{4,5},{5,6},{6,7},{15,8},{8,9},{9,10... | collective-permute-start | bytes 3145736 | tf_op jit(solution)/shard_map/ppermute | solution.py:15
  7.3 46.1 %copy-start.39 = (bf16[256,128]{0,1:T(8,128)(2,1)}, bf16[256,128]{0,1:T(8,128)(2,1)S(1)}, u32[]{:S(2)}) copy-start(bf16[256,128]{0,1:T(8,128)(2,1)S(1)} %copy.20) | copy-start | bytes 196612
  21.6 20.8 %copy-start.2 = (bf16[256,1024]{1,0:T(8,128)(2,1)S(1)}, bf16[256,1024]{1,0:T(8,128)(2,1)}, u32[]{:S(2)}) copy-start(bf16[256,1024]{1,0:T(8,128)(2,1)} %param.6) | copy-start | bytes 1572868
  21.7 20.8 %copy-start.3 = (bf16[256,1024]{1,0:T(8,128)(2,1)S(1)}, bf16[256,1024]{1,0:T(8,128)(2,1)}, u32[]{:S(2)}) copy-start(bf16[256,1024]{1,0:T(8,128)(2,1)} %param.5) | copy-start | bytes 1572868
  54.9 1.4 copy-start.40
  55.4 1.6 %copy-start.38 = (bf16[256,128]{0,1:T(8,128)(2,1)S(1)}, bf16[256,128]{0,1:T(8,128)(2,1)}, u32[]{:S(2)}) copy-start(bf16[256,128]{0,1:T(8,128)(2,1)} %copy.26) | copy-start | bytes 196612
  59.0 2.0 %copy-start.31 = (bf16[768,128]{1,0:T(8,128)(2,1)S(1)}, bf16[768,128]{1,0:T(8,128)(2,1)}, u32[]{:S(2)}) copy-start(bf16[768,128]{1,0:T(8,128)(2,1)} %get-tuple-element.20) | copy-start | bytes 589828
  59.0 2.2 %copy-start.32 = (bf16[768,128]{1,0:T(8,128)(2,1)S(1)}, bf16[768,128]{1,0:T(8,128)(2,1)}, u32[]{:S(2)}) copy-start(bf16[768,128]{1,0:T(8,128)(2,1)} %get-tuple-element.12) | copy-start | bytes 589828
  59.0 2.3 %copy-start.37 = (bf16[256,128]{0,1:T(8,128)(2,1)S(1)}, bf16[256,128]{0,1:T(8,128)(2,1)}, u32[]{:S(2)}) copy-start(bf16[256,128]{0,1:T(8,128)(2,1)} %copy.32) | copy-start | bytes 196612
  64.2 2.0 %copy-start.29 = (bf16[768,128]{1,0:T(8,128)(2,1)S(1)}, bf16[768,128]{1,0:T(8,128)(2,1)}, u32[]{:S(2)}) copy-start(bf16[768,128]{1,0:T(8,128)(2,1)} %get-tuple-element.19) | copy-start | bytes 589828
  64.2 2.2 %copy-start.30 = (bf16[768,128]{1,0:T(8,128)(2,1)S(1)}, bf16[768,128]{1,0:T(8,128)(2,1)}, u32[]{:S(2)}) copy-start(bf16[768,128]{1,0:T(8,128)(2,1)} %get-tuple-element.11) | copy-start | bytes 589828
  64.3 2.3 %copy-start.36 = (bf16[256,128]{0,1:T(8,128)(2,1)S(1)}, bf16[256,128]{0,1:T(8,128)(2,1)}, u32[]{:S(2)}) copy-start(bf16[256,128]{0,1:T(8,128)(2,1)} %copy.38) | copy-start | bytes 196612
  69.6 2.1 %copy-start.27 = (bf16[768,128]{1,0:T(8,128)(2,1)S(1)}, bf16[768,128]{1,0:T(8,128)(2,1)}, u32[]{:S(2)}) copy-start(bf16[768,128]{1,0:T(8,128)(2,1)} %get-tuple-element.18) | copy-start | bytes 589828
  69.6 2.2 %copy-start.28 = (bf16[768,128]{1,0:T(8,128)(2,1)S(1)}, bf16[768,128]{1,0:T(8,128)(2,1)}, u32[]{:S(2)}) copy-start(bf16[768,128]{1,0:T(8,128)(2,1)} %get-tuple-element.10) | copy-start | bytes 589828
  69.7 2.4 %copy-start.35 = (bf16[256,128]{0,1:T(8,128)(2,1)S(1)}, bf16[256,128]{0,1:T(8,128)(2,1)}, u32[]{:S(2)}) copy-start(bf16[256,128]{0,1:T(8,128)(2,1)} %copy.44) | copy-start | bytes 196612
  74.9 2.0 %copy-start.25 = (bf16[768,128]{1,0:T(8,128)(2,1)S(1)}, bf16[768,128]{1,0:T(8,128)(2,1)}, u32[]{:S(2)}) copy-start(bf16[768,128]{1,0:T(8,128)(2,1)} %get-tuple-element.17) | copy-start | bytes 589828
  75.8 1.3 copy-start.26
  77.0 4.5 %copy-start.43 = (bf16[2,64,256]{2,1,0:T(8,128)(2,1)S(1)}, bf16[2,64,256]{2,1,0:T(8,128)(2,1)}, u32[]{:S(2)}) copy-start(bf16[2,64,256]{2,1,0:T(8,128)(2,1)} %fusion.49) | copy-start | bytes 196612
  79.7 3.6 %copy-start.44 = (bf16[2,64,256]{2,1,0:T(8,128)(2,1)S(1)}, bf16[2,64,256]{2,1,0:T(8,128)(2,1)}, u32[]{:S(2)}) copy-start(bf16[2,64,256]{2,1,0:T(8,128)(2,1)} %fusion.50) | copy-start | bytes 196612
  80.6 4.4 %copy-start.4 = (f32[2,768,64]{1,2,0:T(8,128)S(1)}, f32[2,768,64]{1,2,0:T(8,128)}, u32[]{:S(2)}) copy-start(f32[2,768,64]{1,2,0:T(8,128)} %convolution_multiply_fusion.12) | copy-start | bytes 1179652
  82.2 2.9 %copy-start.45 = (bf16[2,64,256]{2,1,0:T(8,128)(2,1)S(1)}, bf16[2,64,256]{2,1,0:T(8,128)(2,1)}, u32[]{:S(2)}) copy-start(bf16[2,64,256]{2,1,0:T(8,128)(2,1)} %fusion.51) | copy-start | bytes 196612
  83.1 3.6 %copy-start.8 = (f32[2,768,64]{1,2,0:T(8,128)S(1)}, f32[2,768,64]{1,2,0:T(8,128)}, u32[]{:S(2)}) copy-start(f32[2,768,64]{1,2,0:T(8,128)} %convolution_multiply_fusion.11) | copy-start | bytes 1179652
  84.0 4.5 %copy-start.5 = (f32[2,768,64]{1,2,0:T(8,128)S(1)}, f32[2,768,64]{1,2,0:T(8,128)}, u32[]{:S(2)}) copy-start(f32[2,768,64]{1,2,0:T(8,128)} %fusion.79) | copy-start | bytes 1179652
  85.0 4.5 %copy-start.10 = (f32[2,768,64]{1,2,0:T(8,128)S(1)}, f32[2,768,64]{1,2,0:T(8,128)}, u32[]{:S(2)}) copy-start(f32[2,768,64]{1,2,0:T(8,128)} %convolution_multiply_fusion.10) | copy-start | bytes 1179652
  85.8 5.4 %copy-start.9 = (f32[2,768,64]{1,2,0:T(8,128)S(1)}, f32[2,768,64]{1,2,0:T(8,128)}, u32[]{:S(2)}) copy-start(f32[2,768,64]{1,2,0:T(8,128)} %fusion.76) | copy-start | bytes 1179652
  88.5 6.3 %copy-start.12 = (f32[2,768,64]{1,2,0:T(8,128)S(1)}, f32[2,768,64]{1,2,0:T(8,128)}, u32[]{:S(2)}) copy-start(f32[2,768,64]{1,2,0:T(8,128)} %fusion.73) | copy-start | bytes 1179652
  89.6 6.2 %copy-start.33 = (bf16[256,128]{0,1:T(8,128)(2,1)S(1)}, bf16[256,128]{0,1:T(8,128)(2,1)}, u32[]{:S(2)}) copy-start(bf16[256,128]{0,1:T(8,128)(2,1)} %copy.50) | copy-start | bytes 196612
  99.0 5.0 %copy-start.11 = (f32[768,128]{1,0:T(8,128)S(1)}, f32[768,128]{1,0:T(8,128)}, u32[]{:S(2)}) copy-start(f32[768,128]{1,0:T(8,128)} %copy.87) | copy-start | bytes 1179652
  104.0 1.2 copy-start.13
  104.0 1.3 copy-start.15
  104.0 1.4 copy-start.16
  104.1 1.4 copy-start.17
  105.3 1.1 copy-start.19
  106.4 1.7 %copy-start = (f32[768,1024]{1,0:T(8,128)}, f32[768,1024]{1,0:T(8,128)S(1)}, u32[]{:S(2)}) copy-start(f32[768,1024]{1,0:T(8,128)S(1)} %constant_dynamic-update-slice_fusion.16) | copy-start | bytes 9437188
  108.1 1.1 copy-start.7
  110.4 1.7 %copy-start.1 = (f32[768,1024]{1,0:T(8,128)}, f32[768,1024]{1,0:T(8,128)S(1)}, u32[]{:S(2)}) copy-start(f32[768,1024]{1,0:T(8,128)S(1)} %constant_dynamic-update-slice_fusion.8) | copy-start | bytes 9437188
  113.2 18.8 %collective-permute-start.3 = (bf16[2,256,1024]{2,1,0:T(8,128)(2,1)}, bf16[2,256,1024]{2,1,0:T(8,128)(2,1)S(1)}, u32[]{:S(2)}, u32[]{:S(2)}) collective-permute-start(bf16[2,256,1024]{2,1,0:T(8,128)(2,1)} %pad_maximum_fusion.4), channel_id=1, source_target_pairs={{8,0},{16,8},{24,16},{32,24},{40,32},{48,40},{56,48},{64,56},{72,6... | collective-permute-start | bytes 3145736 | tf_op jit(solution)/shard_map/ppermute | solution.py:15
  113.2 3.9 %copy-start.46 = (bf16[256,128]{1,0:T(8,128)(2,1)S(1)}, bf16[256,128]{1,0:T(8,128)(2,1)}, u32[]{:S(2)}) copy-start(bf16[256,128]{1,0:T(8,128)(2,1)} %copy.55) | copy-start | bytes 196612
  113.2 3.9 %copy-start.47 = (bf16[256,128]{1,0:T(8,128)(2,1)S(1)}, bf16[256,128]{1,0:T(8,128)(2,1)}, u32[]{:S(2)}) copy-start(bf16[256,128]{1,0:T(8,128)(2,1)} %copy.56) | copy-start | bytes 196612
  113.2 3.9 %copy-start.48 = (bf16[256,128]{1,0:T(8,128)(2,1)S(1)}, bf16[256,128]{1,0:T(8,128)(2,1)}, u32[]{:S(2)}) copy-start(bf16[256,128]{1,0:T(8,128)(2,1)} %copy.57) | copy-start | bytes 196612
  113.2 4.0 %copy-start.49 = (bf16[256,128]{1,0:T(8,128)(2,1)S(1)}, bf16[256,128]{1,0:T(8,128)(2,1)}, u32[]{:S(2)}) copy-start(bf16[256,128]{1,0:T(8,128)(2,1)} %copy.58) | copy-start | bytes 196612
  113.2 4.0 %copy-start.50 = (bf16[256,128]{1,0:T(8,128)(2,1)S(1)}, bf16[256,128]{1,0:T(8,128)(2,1)}, u32[]{:S(2)}) copy-start(bf16[256,128]{1,0:T(8,128)(2,1)} %copy.59) | copy-start | bytes 196612
  113.2 4.0 %copy-start.51 = (bf16[256,128]{1,0:T(8,128)(2,1)S(1)}, bf16[256,128]{1,0:T(8,128)(2,1)}, u32[]{:S(2)}) copy-start(bf16[256,128]{1,0:T(8,128)(2,1)} %copy.60) | copy-start | bytes 196612
  114.3 25.9 %collective-permute-start.2 = (bf16[2,256,1024]{2,1,0:T(8,128)(2,1)}, bf16[2,256,1024]{2,1,0:T(8,128)(2,1)S(1)}, u32[]{:S(2)}, u32[]{:S(2)}) collective-permute-start(bf16[2,256,1024]{2,1,0:T(8,128)(2,1)} %pad_maximum_fusion.3), channel_id=1, source_target_pairs={{1,0},{2,1},{3,2},{4,3},{5,4},{6,5},{7,6},{0,7},{9,8},{10,9},{11,1... | collective-permute-start | bytes 3145736 | tf_op jit(solution)/shard_map/ppermute | solution.py:15
  118.1 14.1 %copy-start.52 = (bf16[256,1024]{1,0:T(8,128)(2,1)}, bf16[256,1024]{1,0:T(8,128)(2,1)S(1)}, u32[]{:S(2)}) copy-start(bf16[256,1024]{1,0:T(8,128)(2,1)S(1)} %constant_dynamic-update-slice_fusion) | copy-start | bytes 1572868
  (9 other events, 8.1 us)
where the time goes:
time: 145 us; the launch traced here: 144 us
  waiting for transfers between devices  49.3 us (34%)
  local copies, waits for them, and re-layouts  48.2 us (33%)
  matrix products  29.7 us (20%)
  other arithmetic  10.1 us (7%)
  starting transfers between devices  4.48 us (3%)
  between operations  1.74 us (1%)
    ppermute x4, waiting for transfers between devices, shifted(): return lax.ppermute(block, axis, route)  49.3 us
    slice x36, local copies, waits for them, and re-layouts, heads_of(): piece = array[:, start:start + width_cols]  13.6 us
    unnamed x127, local copies, waits for them, and re-layouts  9.42 us
    reshape x8, local copies, waits for them, and re-layouts, local(): grad_q_parts.append(grad_q.reshape(rows, group_cols))  8.56 us
    reshape x8, local copies, waits for them, and re-layouts, local(): grad_v_parts.append(grad_v.reshape(keep, group_cols))  8.37 us
    dot_general x8, matrix products, group_window(): jnp.einsum('hts,thd->shd', dscore, q_group, preferred_element_type=jnp.fl...  6.74 us
    dot_general x8, matrix products, group_window(): jnp.einsum('hts,shd->thd', dscore, k_group, preferred_element_type=jnp.fl...  6.46 us
    dot_general x8, matrix products, group_window(): jnp.einsum('hts,thd->shd', prob_low, do_group, preferred_element_type=jnp...  6.21 us
  transfers between devices with their start and end apart: 4, of which 4 were waited for; matrix products, arithmetic and copies ran while one was open for 8% of the time, Pallas kernels for 0%

commit v1 on v0

v1 whole, which is shorter than its diff:
```python
import functools

import jax
import jax.numpy as jnp
from jax import lax
from jax.experimental import pallas as pl
from jax.experimental.pallas import tpu as pltpu
from jax.sharding import PartitionSpec as P

HEAD = 64
COLS = 128
MESH = pl.DeviceIdType.MESH
AHEAD = 2
LAG_C = 1
LAG_B = 2
LAG_E = 4
NT = (((1,), (1,)), ((), ()))


def kernel(
    outer_size, inner_size, groups, rows,
    q_hbm, k_hbm, v_hbm, do_hbm,
    dq_out, dk_out, dv_out,
    qd, kv, km, vm, kt, e_all, dp_all, p_low, ds_low,
    part, part_in, total, total_in, dq_own, dq_send, dq_in,
    load_sem, qd_send, qd_recv, part_send, part_recv,
    total_send, total_recv, dq_ssem, dq_rsem,
):
    o = lax.axis_index("outer")
    i = lax.axis_index("inner")
    before = [(o, lax.rem(i + inner_size - 1, inner_size)), (lax.rem(o + outer_size - 1, outer_size), i)]
    after = [(o, lax.rem(i + 1, inner_size)), (lax.rem(o + 1, outer_size), i)]

    def load_qd(g, which):
        src = (q_hbm, do_hbm)[which]
        return pltpu.make_async_copy(src.at[:, pl.ds(g * COLS, COLS)], qd.at[g, which, 0], load_sem.at[which, g])

    def load_kv(g, which):
        src = (k_hbm, v_hbm)[which]
        return pltpu.make_async_copy(src.at[:, pl.ds(g * COLS, COLS)], kv.at[g, which], load_sem.at[2 + which, g])

    def send_qd(g, r):
        return pltpu.make_async_remote_copy(
            qd.at[g, :, 0], qd.at[g, :, r + 1], qd_send.at[r, g], qd_recv.at[r, g],
            device_id=before[r], device_id_type=MESH)

    def send_part(g, r):
        return pltpu.make_async_remote_copy(
            part.at[g, r + 1], part_in.at[g, r], part_send.at[r, g], part_recv.at[r, g],
            device_id=after[r], device_id_type=MESH)

    def send_total(g, r):
        return pltpu.make_async_remote_copy(
            total.at[g], total_in.at[g, r], total_send.at[r, g], total_recv.at[r, g],
            device_id=before[r], device_id_type=MESH)

    def send_dq(g, r):
        return pltpu.make_async_remote_copy(
            dq_send.at[g, r], dq_in.at[g, r], dq_ssem.at[r, g], dq_rsem.at[r, g],
            device_id=after[r], device_id_type=MESH)

    for g in range(groups):
        for which in range(2):
            load_qd(g, which).start()
    for g in range(groups):
        for which in range(2):
            load_kv(g, which).start()

    barrier = pltpu.get_barrier_semaphore()
    for device in before + after:
        pl.semaphore_signal(barrier, inc=1, device_id=device, device_id_type=MESH)
    pl.semaphore_wait(barrier, 4)

    def start_group(g):
        for which in range(2):
            load_qd(g, which).wait()
        for r in range(2):
            send_qd(g, r).start()

    for g in range(AHEAD):
        start_group(g)

    lane = lax.broadcasted_iota(jnp.int32, (1, COLS), 1)
    first = lane < HEAD
    low = jnp.where(first, 1.0, 0.0)
    high = 1.0 - low
    scale = HEAD ** -0.5

    def prepare(g, carry):
        for which in range(2):
            load_kv(g, which).wait()
        k = kv[g, 0].astype(jnp.float32) * scale
        v = kv[g, 1].astype(jnp.float32)
        k_low, k_high = k * low, k * high
        km[g, 0] = k_low.astype(jnp.bfloat16)
        km[g, 1] = k_high.astype(jnp.bfloat16)
        vm[g, 0] = (v * low).astype(jnp.bfloat16)
        vm[g, 1] = (v * high).astype(jnp.bfloat16)
        kt[g, 0] = k_low.T.astype(jnp.bfloat16)
        kt[g, 1] = k_high.T.astype(jnp.bfloat16)
        return carry

    lax.fori_loop(0, groups, prepare, 0)

    def scores(g, r):
        q = qd[g, 0, r]
        do = qd[g, 1, r]
        for h in range(2):
            s = lax.dot_general(km[g, h], q, NT, preferred_element_type=jnp.float32)
            dp = lax.dot_general(vm[g, h], do, NT, preferred_element_type=jnp.float32)
            top = jnp.max(s, axis=0, keepdims=True)
            e = jnp.exp(s - top)
            e_all[g, r, h] = e
            dp_all[g, r, h] = dp
            part[g, r, pl.ds(h, 1)] = top
            part[g, r, pl.ds(2 + h, 1)] = jnp.sum(e, axis=0, keepdims=True)
            part[g, r, pl.ds(4 + h, 1)] = jnp.sum(e * dp, axis=0, keepdims=True)

    def combine(g):
        for r in range(2):
            send_part(g, r).wait_recv()
        parts = [part[g, 0], part_in[g, 0], part_in[g, 1]]
        tops = [x[0:2] for x in parts]
        top = jnp.maximum(jnp.maximum(tops[0], tops[1]), tops[2])
        weights = [jnp.exp(x - top) for x in tops]
        norm = sum(w * x[2:4] for w, x in zip(weights, parts))
        dots = sum(w * x[4:6] for w, x in zip(weights, parts))
        total[g, 0:2] = top + jnp.log(norm)
        total[g, 2:4] = dots / norm
        for r in range(2):
            send_total(g, r).start()

    def gradients(g):
        for r in range(2):
            send_total(g, r).wait_recv()
        for r in (1, 2, 0):
            sums = total[g] if r == 0 else total_in[g, r - 1]
            for h in range(2):
                factor = jnp.exp(part[g, r, pl.ds(h, 1)] - sums[h:h + 1])
                p = e_all[g, r, h] * factor
                p_low[h, :, r * rows:(r + 1) * rows] = p.astype(jnp.bfloat16)
                ds = p * (dp_all[g, r, h] - sums[2 + h:3 + h])
                ds_low[h, :, r * rows:(r + 1) * rows] = ds.astype(jnp.bfloat16)
            columns = slice(r * rows, (r + 1) * rows)
            dq = jnp.dot(kt[g, 0], ds_low[0, :, columns], preferred_element_type=jnp.float32)
            dq = dq + jnp.dot(kt[g, 1], ds_low[1, :, columns], preferred_element_type=jnp.float32)
            if r == 0:
                dq_own[g] = dq
            else:
                dq_send[g, r - 1] = dq.astype(jnp.bfloat16)
                send_dq(g, r - 1).start()
        columns = pl.ds(pl.multiple_of(g * COLS, COLS), COLS)
        q = qd[g, 0].reshape(3 * rows, COLS)
        do = qd[g, 1].reshape(3 * rows, COLS)
        dv = [jnp.dot(p_low[h], do, preferred_element_type=jnp.float32) for h in range(2)]
        dv_out[:, columns] = jnp.where(first, dv[0], dv[1]).astype(jnp.bfloat16)
        dk = [jnp.dot(ds_low[h], q, preferred_element_type=jnp.float32) for h in range(2)]
        dk_out[:, columns] = (jnp.where(first, dk[0], dk[1]) * scale).astype(jnp.bfloat16)

    def finish(g):
        for r in range(2):
            send_dq(g, r).wait_recv()
        dq = dq_own[g] + dq_in[g, 0].astype(jnp.float32) + dq_in[g, 1].astype(jnp.float32)
        columns = pl.ds(pl.multiple_of(g * COLS, COLS), COLS)
        dq_out[:, columns] = dq.T.astype(jnp.bfloat16)

    def step(t, carry):
        @pl.when(t < groups)
        def _():
            scores(t, 0)
            for r in (1, 0):
                send_qd(t, r).wait_recv()
                scores(t, r + 1)
                send_part(t, r).start()

        @pl.when(t < groups - AHEAD)
        def _():
            start_group(t + AHEAD)

        @pl.when((t >= LAG_C) & (t < groups + LAG_C))
        def _():
            combine(t - LAG_C)

        @pl.when((t >= LAG_B) & (t < groups + LAG_B))
        def _():
            gradients(t - LAG_B)

        @pl.when((t >= LAG_E) & (t < groups + LAG_E))
        def _():
            finish(t - LAG_E)

        return carry

    lax.fori_loop(0, groups + max(LAG_B, LAG_C, LAG_E), step, 0)

    def drain(g, carry):
        for r in range(2):
            send_qd(g, r).wait_send()
            send_part(g, r).wait_send()
            send_total(g, r).wait_send()
            send_dq(g, r).wait_send()
        return carry

    lax.fori_loop(0, groups, drain, 0)


def local(outer_size, inner_size, queries, keys, values, d_output):
    rows, width = queries.shape
    groups = width // COLS
    block = jax.ShapeDtypeStruct((rows, width), jnp.bfloat16)
    low, wide = jnp.bfloat16, jnp.float32
    dma = pltpu.SemaphoreType.DMA
    return pl.pallas_call(
        functools.partial(kernel, outer_size, inner_size, groups, rows),
        out_shape=(block, block, block),
        in_specs=[pl.BlockSpec(memory_space=pl.ANY)] * 4,
        out_specs=[pl.BlockSpec(memory_space=pltpu.VMEM)] * 3,
        scratch_shapes=[
            pltpu.VMEM((groups, 2, 3, rows, COLS), low),
            pltpu.VMEM((groups, 2, rows, COLS), low),
            pltpu.VMEM((groups, 2, rows, COLS), low),
            pltpu.VMEM((groups, 2, rows, COLS), low),
            pltpu.VMEM((groups, 2, COLS, rows), low),
            pltpu.VMEM((groups, 3, 2, rows, rows), wide),
            pltpu.VMEM((groups, 3, 2, rows, rows), wide),
            pltpu.VMEM((2, rows, 3 * rows), low),
            pltpu.VMEM((2, rows, 3 * rows), low),
            pltpu.VMEM((groups, 3, 8, rows), wide),
            pltpu.VMEM((groups, 2, 8, rows), wide),
            pltpu.VMEM((groups, 8, rows), wide),
            pltpu.VMEM((groups, 2, 8, rows), wide),
            pltpu.VMEM((groups, COLS, rows), wide),
            pltpu.VMEM((groups, 2, COLS, rows), low),
            pltpu.VMEM((groups, 2, COLS, rows), low),
            dma((4, groups)),
            dma((2, groups)), dma((2, groups)),
            dma((2, groups)), dma((2, groups)),
            dma((2, groups)), dma((2, groups)),
            dma((2, groups)), dma((2, groups)),
        ],
        compiler_params=pltpu.CompilerParams(
            collective_id=0, has_side_effects=True, vmem_limit_bytes=58 * 2**20),
    )(queries, keys, values, d_output)


def solution(mesh):
    spec = P(("outer", "inner"), None)
    return jax.shard_map(
        functools.partial(local, mesh.shape["outer"], mesh.shape["inner"]),
        mesh=mesh, in_specs=(spec,) * 4, out_specs=(spec,) * 3, check_vma=False)
```

time: 145 us -> 78.4 us (0.54)
  the two profiles are of different devices: /device:TPU:0 before, /device:TPU:24 now
where the time goes in v1:
time: 78.4 us; the launch traced here: 78.2 us
  Pallas kernels  73.6 us (94%)
  local copies, waits for them, and re-layouts  3.95 us (5%)
    pallas_call x1, Pallas kernels, local(): pl.pallas_call(functools.partial(kernel, outer_size, inner_size, groups,...  73.6 us
    unnamed x7, local copies, waits for them, and re-layouts  3.95 us

profile of v1, /device:TPU:24, one launch (start us, length us, event | category | flops | bytes accessed | tf_op | source)
XLA Modules:
  0.0 78.2 jit_solution(16035965896191725746)
XLA Ops:
  0.6 73.6 %shard_map.67 = (bf16[256,1024]{1,0:T(8,128)(2,1)}, bf16[256,1024]{1,0:T(8,128)(2,1)}, bf16[256,1024]{1,0:T(8,128)(2,1)}) custom-call(bf16[256,1024]{1,0:T(8,128)(2,1)} %q_hbm.1, bf16[256,1024]{1,0:T(8,128)(2,1)} %k_hbm.1, bf16[256,1024]{1,0:T(8,128)(2,1)} %v_hbm.1, bf16[256,1024]{1,0:T(8,128)(2,1)} %do_hbm.1), custom_call_target="tpu_custom_call" | custom-call | tf_op jit(solution)/shard_map/pallas_call | solution.py:213
  74.2 0.0 copy-start.1
  74.2 1.9 %copy.10 = bf16[256,1024]{1,0:T(8,128)(2,1)} copy(bf16[256,1024]{1,0:T(8,128)(2,1)} %get-tuple-element.6) | data formatting | bytes 1048576
  76.2 0.0 copy-done.1
  76.2 0.0 copy-start
  76.2 0.8 %copy.11 = bf16[256,1024]{1,0:T(8,128)(2,1)} copy(bf16[256,1024]{1,0:T(8,128)(2,1)S(1)} %copy-done.1) | data formatting | bytes 1048576
  77.0 0.4 copy-done
  77.4 0.8 %copy.12 = bf16[256,1024]{1,0:T(8,128)(2,1)} copy(bf16[256,1024]{1,0:T(8,128)(2,1)S(1)} %copy-done) | data formatting | bytes 1048576
Async XLA Ops:
  74.2 1.9 %copy-start.1 = (bf16[256,1024]{1,0:T(8,128)(2,1)S(1)}, bf16[256,1024]{1,0:T(8,128)(2,1)}, u32[]{:S(2)}) copy-start(bf16[256,1024]{1,0:T(8,128)(2,1)} %get-tuple-element.7) | copy-start | bytes 1572868
  76.2 1.2 %copy-start = (bf16[256,1024]{1,0:T(8,128)(2,1)S(1)}, bf16[256,1024]{1,0:T(8,128)(2,1)}, u32[]{:S(2)}) copy-start(bf16[256,1024]{1,0:T(8,128)(2,1)} %get-tuple-element.8) | copy-start | bytes 1572868

commit v2 on v1

v2 whole, which is shorter than its diff:
```python
import functools

import jax
import jax.numpy as jnp
from jax import lax
from jax.experimental import pallas as pl
from jax.experimental.pallas import tpu as pltpu
from jax.sharding import PartitionSpec as P

HEAD = 64
COLS = 128
MESH = pl.DeviceIdType.MESH
AHEAD = 2
BATCHES = ((0, 4), (4, 4))
COMBINE = (5, 8)
LAG_B = 6
LAG_K = 10
LAG_E = 10
BACK_LAG = 2
HOP_LEAD = 1
NT = (((1,), (1,)), ((), ()))
RELAYS = {2: (1, 3, 6), 4: (2, 4, 7)}
RELAYED = sum(RELAYS.values(), ())
BACK = {}
BACKED = sum(BACK.values(), ())


def kernel(
    outer_size, inner_size, groups, rows,
    q_hbm, k_hbm, v_hbm, do_hbm,
    dq_out, dk_out, dv_out,
    qd, kv, km, vm, kt, e_all, dp_all, p_low, ds_low,
    part, part_in, total, total_in, dq_own, dq_send, dq_in, passing, passing_back,
    load_sem, qd_send, qd_recv, part_send, part_recv,
    total_send, total_recv, dq_ssem, dq_rsem, hop_send, hop_recv, pass_send,
    back_recv, back_send,
):
    o = lax.axis_index("outer")
    i = lax.axis_index("inner")
    before = [(o, lax.rem(i + inner_size - 1, inner_size)), (lax.rem(o + outer_size - 1, outer_size), i)]
    after = [(o, lax.rem(i + 1, inner_size)), (lax.rem(o + 1, outer_size), i)]

    def load_qd(g, which):
        src = (q_hbm, do_hbm)[which]
        return pltpu.make_async_copy(src.at[:, pl.ds(g * COLS, COLS)], qd.at[g, which, 0], load_sem.at[which, g])

    def load_kv(g, which):
        src = (k_hbm, v_hbm)[which]
        return pltpu.make_async_copy(src.at[:, pl.ds(g * COLS, COLS)], kv.at[g, which], load_sem.at[2 + which, g])

    def send_qd(g, r):
        return pltpu.make_async_remote_copy(
            qd.at[g, :, 0], qd.at[g, :, r + 1], qd_send.at[r, g], qd_recv.at[r, g],
            device_id=before[r], device_id_type=MESH)

    half = outer_size // 2
    place = lax.rem(o, half)
    base = o - place
    other = lax.rem(base + half, outer_size)
    wraps = place == 0

    def hop_in(g, slot, relay):
        return pltpu.make_async_remote_copy(
            qd.at[g, :, 0], passing.at[slot], hop_send.at[g], hop_recv.at[slot],
            device_id=(other + relay, i), device_id_type=MESH)

    def hop_out(g, slot):
        return pltpu.make_async_remote_copy(
            passing.at[slot], qd.at[g, :, 2], pass_send.at[slot], qd_recv.at[1, g],
            device_id=(base + half - 1, i), device_id_type=MESH)

    def back_in(g, slot, relay):
        return pltpu.make_async_remote_copy(
            dq_send.at[g, 1], passing_back.at[slot], dq_ssem.at[1, g], back_recv.at[slot],
            device_id=(other + relay, i), device_id_type=MESH)

    def back_out(g, slot):
        return pltpu.make_async_remote_copy(
            passing_back.at[slot], dq_in.at[g, 1], back_send.at[slot], dq_rsem.at[1, g],
            device_id=(base, i), device_id_type=MESH)

    def send_part(b, r):
        batch = pl.ds(*BATCHES[b])
        return pltpu.make_async_remote_copy(
            part.at[r + 1, batch], part_in.at[r, batch], part_send.at[r, b], part_recv.at[r, b],
            device_id=after[r], device_id_type=MESH)

    def send_total(b, r):
        batch = pl.ds(*BATCHES[b])
        return pltpu.make_async_remote_copy(
            total.at[batch], total_in.at[r, batch], total_send.at[r, b], total_recv.at[r, b],
            device_id=before[r], device_id_type=MESH)

    def send_dq(g, r):
        return pltpu.make_async_remote_copy(
            dq_send.at[g, r], dq_in.at[g, r], dq_ssem.at[r, g], dq_rsem.at[r, g],
            device_id=after[r], device_id_type=MESH)

    for g in range(groups):
        for which in range(2):
            load_qd(g, which).start()
    for g in range(groups):
        for which in range(2):
            load_kv(g, which).start()

    barrier = pltpu.get_barrier_semaphore()
    for device in before + after:
        pl.semaphore_signal(barrier, inc=1, device_id=device, device_id_type=MESH)
    peers = {n: 4 for n in range(half)}
    for relay in RELAYS:
        @pl.when(place == relay)
        def _():
            pl.semaphore_signal(barrier, inc=1, device_id=(other, i), device_id_type=MESH)

        @pl.when(place == half - 1)
        def _():
            pl.semaphore_signal(barrier, inc=1, device_id=(base + relay, i), device_id_type=MESH)

        peers[0] += 1
        peers[relay] += 1
    for relay in BACK:
        @pl.when(place == relay)
        def _():
            pl.semaphore_signal(barrier, inc=1, device_id=(other + half - 1, i), device_id_type=MESH)

        @pl.when(place == 0)
        def _():
            pl.semaphore_signal(barrier, inc=1, device_id=(base + relay, i), device_id_type=MESH)

        peers[half - 1] += 1
        peers[relay] += 1
    for count in sorted(set(peers.values())):
        @pl.when(functools.reduce(lambda a, b: a | b, [place == n for n in range(half) if peers[n] == count]))
        def _():
            pl.semaphore_wait(barrier, count)

    def among(g, listed):
        return functools.reduce(lambda a, b: a | b, [g == n for n in listed], g < 0)

    def start_group(g):
        send_qd(g, 0).start()

        @pl.when(jnp.logical_not(wraps & among(g, RELAYED)))
        def _():
            send_qd(g, 1).start()

    for g in range(groups):
        for which in range(2):
            load_qd(g, which).wait()
        if g < AHEAD:
            start_group(jnp.int32(g))

    @pl.when(wraps)
    def _():
        for g in sorted(RELAYED):
            for relay, listed in RELAYS.items():
                if g in listed:
                    hop_in(g, listed.index(g), relay).start()

    lane = lax.broadcasted_iota(jnp.int32, (1, COLS), 1)
    first = lane < HEAD
    low = jnp.where(first, 1.0, 0.0)
    high = 1.0 - low
    scale = HEAD ** -0.5

    def prepare(g, carry):
        for which in range(2):
            load_kv(g, which).wait()
        k = kv[g, 0].astype(jnp.float32) * scale
        v = kv[g, 1].astype(jnp.float32)
        k_low, k_high = k * low, k * high
        km[g, 0] = k_low.astype(jnp.bfloat16)
        km[g, 1] = k_high.astype(jnp.bfloat16)
        vm[g, 0] = (v * low).astype(jnp.bfloat16)
        vm[g, 1] = (v * high).astype(jnp.bfloat16)
        kt[g, 0] = k_low.T.astype(jnp.bfloat16)
        kt[g, 1] = k_high.T.astype(jnp.bfloat16)
        return carry

    lax.fori_loop(0, groups, prepare, 0)

    def scores(g, r):
        q = qd[g, 0, r]
        do = qd[g, 1, r]
        for h in range(2):
            s = lax.dot_general(km[g, h], q, NT, preferred_element_type=jnp.float32)
            dp = lax.dot_general(vm[g, h], do, NT, preferred_element_type=jnp.float32)
            top = jnp.max(s, axis=0, keepdims=True)
            e = jnp.exp(s - top)
            e_all[g, r, h] = e
            dp_all[g, r, h] = dp
            part[r, g, pl.ds(h, 1)] = top
            part[r, g, pl.ds(2 + h, 1)] = jnp.sum(e, axis=0, keepdims=True)
            part[r, g, pl.ds(4 + h, 1)] = jnp.sum(e * dp, axis=0, keepdims=True)

    def combine(b):
        for r in range(2):
            send_part(b, r).wait_recv()

        def one(g, carry):
            parts = [part[0, g], part_in[0, g], part_in[1, g]]
            tops = [x[0:2] for x in parts]
            top = jnp.maximum(jnp.maximum(tops[0], tops[1]), tops[2])
            weights = [jnp.exp(x - top) for x in tops]
            norm = sum(w * x[2:4] for w, x in zip(weights, parts))
            dots = sum(w * x[4:6] for w, x in zip(weights, parts))
            total[g, 0:2] = top + jnp.log(norm)
            total[g, 2:4] = dots / norm
            return carry

        first, count = BATCHES[b]
        lax.fori_loop(first, first + count, one, 0)
        for r in range(2):
            send_total(b, r).start()

    def gradients(g):
        for b in range(len(BATCHES)):
            @pl.when(g == BATCHES[b][0])
            def _():
                for r in range(2):
                    send_total(b, r).wait_recv()
        for r in (1, 2, 0):
            sums = total[g] if r == 0 else total_in[r - 1, g]
            for h in range(2):
                factor = jnp.exp(part[r, g, pl.ds(h, 1)] - sums[h:h + 1])
                p = e_all[g, r, h] * factor
                p_low[g, h, :, r * rows:(r + 1) * rows] = p.astype(jnp.bfloat16)
                ds = p * (dp_all[g, r, h] - sums[2 + h:3 + h])
                ds_low[g, h, :, r * rows:(r + 1) * rows] = ds.astype(jnp.bfloat16)
            columns = slice(r * rows, (r + 1) * rows)
            dq = jnp.dot(kt[g, 0], ds_low[g, 0, :, columns], preferred_element_type=jnp.float32)
            dq = dq + jnp.dot(kt[g, 1], ds_low[g, 1, :, columns], preferred_element_type=jnp.float32)
            if r == 0:
                dq_own[g] = dq
            else:
                dq_send[g, r - 1] = dq.astype(jnp.bfloat16)
                if r == 1:
                    send_dq(g, 0).start()
                else:
                    @pl.when(jnp.logical_not((place == half - 1) & among(g, BACKED)))
                    def _():
                        send_dq(g, 1).start()

                    for relay, listed in BACK.items():
                        for slot, n in enumerate(listed):
                            @pl.when((place == half - 1) & (g == n))
                            def _():
                                back_in(n, slot, relay).start()
    def key_gradients(g):
        columns = pl.ds(pl.multiple_of(g * COLS, COLS), COLS)
        q = qd[g, 0].reshape(3 * rows, COLS)
        do = qd[g, 1].reshape(3 * rows, COLS)
        dv = [jnp.dot(p_low[g, h], do, preferred_element_type=jnp.float32) for h in range(2)]
        dv_out[:, columns] = jnp.where(first, dv[0], dv[1]).astype(jnp.bfloat16)
        dk = [jnp.dot(ds_low[g, h], q, preferred_element_type=jnp.float32) for h in range(2)]
        dk_out[:, columns] = (jnp.where(first, dk[0], dk[1]) * scale).astype(jnp.bfloat16)

    def finish(g):
        for r in range(2):
            send_dq(g, r).wait_recv()
        dq = dq_own[g] + dq_in[g, 0].astype(jnp.float32) + dq_in[g, 1].astype(jnp.float32)
        columns = pl.ds(pl.multiple_of(g * COLS, COLS), COLS)
        dq_out[:, columns] = dq.T.astype(jnp.bfloat16)

    def step(t, carry):
        @pl.when(t < groups)
        def _():
            scores(t, 0)
            send_qd(t, 1).wait_recv()
            scores(t, 2)

        for relay, listed in RELAYS.items():
            for slot, g in enumerate(listed):
                @pl.when((place == relay) & (t == g - HOP_LEAD))
                def _():
                    hop_in(g, slot, relay).wait_recv()
                    hop_out(g, slot).start()

        @pl.when(t < groups)
        def _():
            send_qd(t, 0).wait_recv()
            scores(t, 1)

        for b in range(len(BATCHES)):
            @pl.when(t == sum(BATCHES[b]) - 1)
            def _():
                for r in range(2):
                    send_part(b, r).start()

        @pl.when(t < groups - AHEAD)
        def _():
            start_group(t + AHEAD)

        for b in range(len(BATCHES)):
            @pl.when(t == COMBINE[b])
            def _():
                combine(b)

        @pl.when((t >= LAG_B) & (t < groups + LAG_B))
        def _():
            gradients(t - LAG_B)

        for relay, listed in BACK.items():
            for slot, n in enumerate(listed):
                @pl.when((place == relay) & (t == n + LAG_B + BACK_LAG))
                def _():
                    back_in(n, slot, relay).wait_recv()
                    back_out(n, slot).start()

        @pl.when((t >= LAG_K) & (t < groups + LAG_K))
        def _():
            key_gradients(t - LAG_K)

        @pl.when((t >= LAG_E) & (t < groups + LAG_E))
        def _():
            finish(t - LAG_E)

        return carry

    lax.fori_loop(0, groups + max(LAG_K, LAG_E), step, 0)

    def drain(g, carry):
        for r in range(2):
            send_dq(g, r).wait_send()
        send_qd(g, 0).wait_send()

        @pl.when(jnp.logical_not(wraps & among(g, RELAYED)))
        def _():
            send_qd(g, 1).wait_send()

        return carry

    lax.fori_loop(0, groups, drain, 0)
    for relay, listed in BACK.items():
        for slot, g in enumerate(listed):
            @pl.when(place == relay)
            def _():
                back_out(g, slot).wait_send()

    for relay, listed in RELAYS.items():
        for slot, g in enumerate(listed):
            @pl.when(wraps)
            def _():
                hop_in(g, slot, relay).wait_send()

            @pl.when(place == relay)
            def _():
                hop_out(g, slot).wait_send()

    for b in range(len(BATCHES)):
        for r in range(2):
            send_part(b, r).wait_send()
            send_total(b, r).wait_send()


def copy_kernel(*refs):
    count = len(refs) // 3
    sems = refs[-1]
    ins, outs, held = refs[:count], refs[count:2 * count], refs[2 * count:3 * count]
    loads = [pltpu.make_async_copy(ins[n], held[n], sems.at[0, n]) for n in range(count)]
    stores = [pltpu.make_async_copy(held[n], outs[n], sems.at[1, n]) for n in range(count)]
    for load in loads:
        load.start()
    for load, store in zip(loads, stores):
        load.wait()
        store.start()
    for store in stores:
        store.wait()


def local(outer_size, inner_size, queries, keys, values, d_output):
    rows, width = queries.shape
    groups = width // COLS
    block = jax.ShapeDtypeStruct((rows, width), jnp.bfloat16)
    low, wide = jnp.bfloat16, jnp.float32
    dma = pltpu.SemaphoreType.DMA
    grads = pl.pallas_call(
        functools.partial(kernel, outer_size, inner_size, groups, rows),
        out_shape=(block, block, block),
        in_specs=[pl.BlockSpec(memory_space=pl.ANY)] * 4,
        out_specs=[pl.BlockSpec(memory_space=pltpu.VMEM)] * 3,
        scratch_shapes=[
            pltpu.VMEM((groups, 2, 3, rows, COLS), low),
            pltpu.VMEM((groups, 2, rows, COLS), low),
            pltpu.VMEM((groups, 2, rows, COLS), low),
            pltpu.VMEM((groups, 2, rows, COLS), low),
            pltpu.VMEM((groups, 2, COLS, rows), low),
            pltpu.VMEM((groups, 3, 2, rows, rows), wide),
            pltpu.VMEM((groups, 3, 2, rows, rows), wide),
            pltpu.VMEM((groups, 2, rows, 3 * rows), low),
            pltpu.VMEM((groups, 2, rows, 3 * rows), low),
            pltpu.VMEM((3, groups, 8, rows), wide),
            pltpu.VMEM((2, groups, 8, rows), wide),
            pltpu.VMEM((groups, 8, rows), wide),
            pltpu.VMEM((2, groups, 8, rows), wide),
            pltpu.VMEM((groups, COLS, rows), wide),
            pltpu.VMEM((groups, 2, COLS, rows), low),
            pltpu.VMEM((groups, 2, COLS, rows), low),
            pltpu.VMEM((3, 2, rows, COLS), low),
            pltpu.VMEM((2, COLS, rows), low),
            dma((4, groups)),
            dma((2, groups)), dma((2, groups)),
            dma((2, groups)), dma((2, groups)),
            dma((2, groups)), dma((2, groups)),
            dma((2, groups)), dma((2, groups)),
            dma((groups,)), dma((3,)), dma((3,)),
            dma((2,)), dma((2,)),
        ],
        compiler_params=pltpu.CompilerParams(
            collective_id=0, has_side_effects=True, vmem_limit_bytes=58 * 2**20),
    )(queries, keys, values, d_output)
    return pl.pallas_call(
        copy_kernel,
        out_shape=(block, block, block),
        in_specs=[pl.BlockSpec(memory_space=pl.ANY)] * 3,
        out_specs=[pl.BlockSpec(memory_space=pl.ANY)] * 3,
        scratch_shapes=[pltpu.VMEM((rows, width), low)] * 3 + [dma((2, 3))],
    )(*grads)


def solution(mesh):
    spec = P(("outer", "inner"), None)
    return jax.shard_map(
        functools.partial(local, mesh.shape["outer"], mesh.shape["inner"]),
        mesh=mesh, in_specs=(spec,) * 4, out_specs=(spec,) * 3, check_vma=False)
```

time: 78.4 us -> 67.2 us (0.86)
  the two profiles are of different devices: /device:TPU:24 before, /device:TPU:0 now
where the time goes in v2:
time: 67.2 us; the launch traced here: 65.9 us
  Pallas kernels  65.2 us (97%)
    pallas_call x1, Pallas kernels, local(): pl.pallas_call(functools.partial(kernel, outer_size, inner_size, groups,...  63 us
    pallas_call x1, Pallas kernels, local(): pl.pallas_call(copy_kernel, out_shape=(block, block, block), in_specs=[pl...  2.23 us

profile of v2, /device:TPU:0, one launch (start us, length us, event | category | flops | bytes accessed | tf_op | source)
XLA Modules:
  0.0 65.9 jit_solution(3852891632113503925)
XLA Ops:
  0.6 63.0 %shard_map.67 = (bf16[256,1024]{1,0:T(8,128)(2,1)}, bf16[256,1024]{1,0:T(8,128)(2,1)}, bf16[256,1024]{1,0:T(8,128)(2,1)}) custom-call(bf16[256,1024]{1,0:T(8,128)(2,1)} %q_hbm.1, bf16[256,1024]{1,0:T(8,128)(2,1)} %k_hbm.1, bf16[256,1024]{1,0:T(8,128)(2,1)} %v_hbm.1, bf16[256,1024]{1,0:T(8,128)(2,1)} %do_hbm.1), custom_call_target="tpu_custom_call" | custom-call | tf_op jit(solution)/shard_map/pallas_call | solution.py:377
  63.6 2.2 %shard_map.68 = (bf16[256,1024]{1,0:T(8,128)(2,1)}, bf16[256,1024]{1,0:T(8,128)(2,1)}, bf16[256,1024]{1,0:T(8,128)(2,1)}) custom-call(bf16[256,1024]{1,0:T(8,128)(2,1)} %get-tuple-element.6.refs_0_, bf16[256,1024]{1,0:T(8,128)(2,1)} %get-tuple-element.7.refs_1_, bf16[256,1024]{1,0:T(8,128)(2,1)} %get-tuple-element.8.refs_2_), custom_call_target="tpu_custom_call" | custom-call | tf_op jit(solution)/shard_map/pallas_call | solution.py:412

commit v3 on v2

--- a/solution.py
+++ b/solution.py
@@ -11,18 +11,14 @@
 COLS = 128
 MESH = pl.DeviceIdType.MESH
 AHEAD = 2
-BATCHES = ((0, 4), (4, 4))
-COMBINE = (5, 8)
+BATCHES = ((0,4),(4,2),(6,2))
 LAG_B = 6
-LAG_K = 10
-LAG_E = 10
-BACK_LAG = 2
+LAG_K = 7
+LAG_E = 8
 HOP_LEAD = 1
 NT = (((1,), (1,)), ((), ()))
 RELAYS = {2: (1, 3, 6), 4: (2, 4, 7)}
 RELAYED = sum(RELAYS.values(), ())
-BACK = {}
-BACKED = sum(BACK.values(), ())
 
 
 def kernel(
@@ -30,15 +26,15 @@
     q_hbm, k_hbm, v_hbm, do_hbm,
     dq_out, dk_out, dv_out,
     qd, kv, km, vm, kt, e_all, dp_all, p_low, ds_low,
-    part, part_in, total, total_in, dq_own, dq_send, dq_in, passing, passing_back,
-    load_sem, qd_send, qd_recv, part_send, part_recv,
-    total_send, total_recv, dq_ssem, dq_rsem, hop_send, hop_recv, pass_send,
-    back_recv, back_send,
+    part, stats, stats_in, dq_own, dq_send, dq_in, passing,
+    load_sem, qd_send, qd_recv, stats_send, stats_recv,
+    dq_ssem, dq_rsem, hop_send, hop_recv, pass_send,
 ):
     o = lax.axis_index("outer")
     i = lax.axis_index("inner")
     before = [(o, lax.rem(i + inner_size - 1, inner_size)), (lax.rem(o + outer_size - 1, outer_size), i)]
     after = [(o, lax.rem(i + 1, inner_size)), (lax.rem(o + 1, outer_size), i)]
+    across = [(before[1][0], after[0][1]), (after[1][0], before[0][1])]
 
     def load_qd(g, which):
         src = (q_hbm, do_hbm)[which]
@@ -69,27 +65,22 @@
             passing.at[slot], qd.at[g, :, 2], pass_send.at[slot], qd_recv.at[1, g],
             device_id=(base + half - 1, i), device_id_type=MESH)
 
-    def back_in(g, slot, relay):
-        return pltpu.make_async_remote_copy(
-            dq_send.at[g, 1], passing_back.at[slot], dq_ssem.at[1, g], back_recv.at[slot],
-            device_id=(other + relay, i), device_id_type=MESH)
-
-    def back_out(g, slot):
-        return pltpu.make_async_remote_copy(
-            passing_back.at[slot], dq_in.at[g, 1], back_send.at[slot], dq_rsem.at[1, g],
-            device_id=(base, i), device_id_type=MESH)
-
-    def send_part(b, r):
-        batch = pl.ds(*BATCHES[b])
-        return pltpu.make_async_remote_copy(
-            part.at[r + 1, batch], part_in.at[r, batch], part_send.at[r, b], part_recv.at[r, b],
-            device_id=after[r], device_id_type=MESH)
-
-    def send_total(b, r):
-        batch = pl.ds(*BATCHES[b])
-        return pltpu.make_async_remote_copy(
-            total.at[batch], total_in.at[r, batch], total_send.at[r, b], total_recv.at[r, b],
-            device_id=before[r], device_id_type=MESH)
+    routes = (
+        (0, before[0], 1, 0),
+        (1, after[0], 0, 0),
+        (1, across[0], 2, 1),
+        (2, across[1], 1, 1),
+        (0, before[1], 2, 0),
+        (2, after[1], 0, 1),
+    )
+
+    def send_stats(b, n):
+        r, device, there, place_there = routes[n]
+        start, count = BATCHES[b]
+        pairs = pl.ds(start // 2, count // 2)
+        return pltpu.make_async_remote_copy(
+            stats.at[r, pairs], stats_in.at[there, place_there, pairs], stats_send.at[n, b], stats_recv.at[n, b],
+            device_id=device, device_id_type=MESH)
 
     def send_dq(g, r):
         return pltpu.make_async_remote_copy(
@@ -104,9 +95,9 @@
             load_kv(g, which).start()
 
     barrier = pltpu.get_barrier_semaphore()
-    for device in before + after:
+    for device in before + after + across:
         pl.semaphore_signal(barrier, inc=1, device_id=device, device_id_type=MESH)
-    peers = {n: 4 for n in range(half)}
+    peers = {n: 6 for n in range(half)}
     for relay in RELAYS:
         @pl.when(place == relay)
         def _():
@@ -117,17 +108,6 @@
             pl.semaphore_signal(barrier, inc=1, device_id=(base + relay, i), device_id_type=MESH)
 
         peers[0] += 1
-        peers[relay] += 1
-    for relay in BACK:
-        @pl.when(place == relay)
-        def _():
-            pl.semaphore_signal(barrier, inc=1, device_id=(other + half - 1, i), device_id_type=MESH)
-
-        @pl.when(place == 0)
-        def _():
-            pl.semaphore_signal(barrier, inc=1, device_id=(base + relay, i), device_id_type=MESH)
-
-        peers[half - 1] += 1
         peers[relay] += 1
     for count in sorted(set(peers.values())):
         @pl.when(functools.reduce(lambda a, b: a | b, [place == n for n in range(half) if peers[n] == count]))
@@ -189,43 +169,39 @@
             e = jnp.exp(s - top)
             e_all[g, r, h] = e
             dp_all[g, r, h] = dp
-            part[r, g, pl.ds(h, 1)] = top
-            part[r, g, pl.ds(2 + h, 1)] = jnp.sum(e, axis=0, keepdims=True)
-            part[r, g, pl.ds(4 + h, 1)] = jnp.sum(e * dp, axis=0, keepdims=True)
-
-    def combine(b):
-        for r in range(2):
-            send_part(b, r).wait_recv()
-
-        def one(g, carry):
-            parts = [part[0, g], part_in[0, g], part_in[1, g]]
-            tops = [x[0:2] for x in parts]
-            top = jnp.maximum(jnp.maximum(tops[0], tops[1]), tops[2])
-            weights = [jnp.exp(x - top) for x in tops]
-            norm = sum(w * x[2:4] for w, x in zip(weights, parts))
-            dots = sum(w * x[4:6] for w, x in zip(weights, parts))
-            total[g, 0:2] = top + jnp.log(norm)
-            total[g, 2:4] = dots / norm
-            return carry
-
-        first, count = BATCHES[b]
-        lax.fori_loop(first, first + count, one, 0)
-        for r in range(2):
-            send_total(b, r).start()
+            norm = jnp.sum(e, axis=0, keepdims=True)
+            part[r, g, pl.ds(h, 1)] = top + jnp.log(norm)
+            part[r, g, pl.ds(2 + h, 1)] = jnp.sum(e * dp, axis=0, keepdims=True) / norm
+            part[r, g, pl.ds(4 + h, 1)] = top
+
+    def share(b):
+        start, count = BATCHES[b]
+        for r in range(3):
+            for g in range(start, start + count, 2):
+                stats[r, g // 2, 0:4] = part[r, g, 0:4]
+                stats[r, g // 2, 4:8] = part[r, g + 1, 0:4]
+        for n in range(len(routes)):
+            send_stats(b, n).start()
 
     def gradients(g):
         for b in range(len(BATCHES)):
             @pl.when(g == BATCHES[b][0])
             def _():
-                for r in range(2):
-                    send_total(b, r).wait_recv()
+                for n in range(len(routes)):
+                    send_stats(b, n).wait_recv()
+
+        odd = lax.rem(g, 2) == 1
         for r in (1, 2, 0):
-            sums = total[g] if r == 0 else total_in[r - 1, g]
+            both = [stats_in[r, n, g // 2] for n in range(2)]
+            parts = [part[r, g, 0:4]] + [jnp.where(odd, x[4:8], x[0:4]) for x in both]
+            top = functools.reduce(jnp.maximum, [x[0:2] for x in parts])
+            lse = top + jnp.log(sum(jnp.exp(x[0:2] - top) for x in parts))
+            delta = sum(jnp.exp(x[0:2] - lse) * x[2:4] for x in parts)
             for h in range(2):
-                factor = jnp.exp(part[r, g, pl.ds(h, 1)] - sums[h:h + 1])
+                factor = jnp.exp(part[r, g, pl.ds(4 + h, 1)] - lse[h:h + 1])
                 p = e_all[g, r, h] * factor
                 p_low[g, h, :, r * rows:(r + 1) * rows] = p.astype(jnp.bfloat16)
-                ds = p * (dp_all[g, r, h] - sums[2 + h:3 + h])
+                ds = p * (dp_all[g, r, h] - delta[h:h + 1])
                 ds_low[g, h, :, r * rows:(r + 1) * rows] = ds.astype(jnp.bfloat16)
             columns = slice(r * rows, (r + 1) * rows)
             dq = jnp.dot(kt[g, 0], ds_low[g, 0, :, columns], preferred_element_type=jnp.float32)
@@ -234,18 +210,8 @@
                 dq_own[g] = dq
             else:
                 dq_send[g, r - 1] = dq.astype(jnp.bfloat16)
-                if r == 1:
-                    send_dq(g, 0).start()
-                else:
-                    @pl.when(jnp.logical_not((place == half - 1) & among(g, BACKED)))
-                    def _():
-                        send_dq(g, 1).start()
-
-                    for relay, listed in BACK.items():
-                        for slot, n in enumerate(listed):
-                            @pl.when((place == half - 1) & (g == n))
-                            def _():
-                                back_in(n, slot, relay).start()
+                send_dq(g, r - 1).start()
+
     def key_gradients(g):
         columns = pl.ds(pl.multiple_of(g * COLS, COLS), COLS)
         q = qd[g, 0].reshape(3 * rows, COLS)
@@ -284,28 +250,15 @@
         for b in range(len(BATCHES)):
             @pl.when(t == sum(BATCHES[b]) - 1)
             def _():
-                for r in range(2):
-                    send_part(b, r).start()
+                share(b)
 
         @pl.when(t < groups - AHEAD)
         def _():
             start_group(t + AHEAD)
 
-        for b in range(len(BATCHES)):
-            @pl.when(t == COMBINE[b])
-            def _():
-                combine(b)
-
         @pl.when((t >= LAG_B) & (t < groups + LAG_B))
         def _():
             gradients(t - LAG_B)
-
-        for relay, listed in BACK.items():
-            for slot, n in enumerate(listed):
-                @pl.when((place == relay) & (t == n + LAG_B + BACK_LAG))
-                def _():
-                    back_in(n, slot, relay).wait_recv()
-                    back_out(n, slot).start()
 
         @pl.when((t >= LAG_K) & (t < groups + LAG_K))
         def _():
@@ -331,12 +284,6 @@
         return carry
 
     lax.fori_loop(0, groups, drain, 0)
-    for relay, listed in BACK.items():
-        for slot, g in enumerate(listed):
-            @pl.when(place == relay)
-            def _():
-                back_out(g, slot).wait_send()
-
     for relay, listed in RELAYS.items():
         for slot, g in enumerate(listed):
             @pl.when(wraps)
@@ -348,9 +295,8 @@
                 hop_out(g, slot).wait_send()
 
     for b in range(len(BATCHES)):
-        for r in range(2):
-            send_part(b, r).wait_send()
-            send_total(b, r).wait_send()
+        for n in range(len(routes)):
+            send_stats(b, n).wait_send()
 
 
 def copy_kernel(*refs):
@@ -390,21 +336,17 @@
             pltpu.VMEM((groups, 2, rows, 3 * rows), low),
             pltpu.VMEM((groups, 2, rows, 3 * rows), low),
             pltpu.VMEM((3, groups, 8, rows), wide),
-            pltpu.VMEM((2, groups, 8, rows), wide),
-            pltpu.VMEM((groups, 8, rows), wide),
-            pltpu.VMEM((2, groups, 8, rows), wide),
+            pltpu.VMEM((3, groups // 2, 8, rows), wide),
+            pltpu.VMEM((3, 2, groups // 2, 8, rows), wide),
             pltpu.VMEM((groups, COLS, rows), wide),
             pltpu.VMEM((groups, 2, COLS, rows), low),
             pltpu.VMEM((groups, 2, COLS, rows), low),
             pltpu.VMEM((3, 2, rows, COLS), low),
-            pltpu.VMEM((2, COLS, rows), low),
             dma((4, groups)),
             dma((2, groups)), dma((2, groups)),
-            dma((2, groups)), dma((2, groups)),
-            dma((2, groups)), dma((2, groups)),
+            dma((6, len(BATCHES))), dma((6, len(BATCHES))),
             dma((2, groups)), dma((2, groups)),
             dma((groups,)), dma((3,)), dma((3,)),
-            dma((2,)), dma((2,)),
         ],
         compiler_params=pltpu.CompilerParams(
             collective_id=0, has_side_effects=True, vmem_limit_bytes=58 * 2**20),

time: 67.2 us -> 61 us (0.908); the launches traced: 65.9 us -> 60.6 us
  Pallas kernels: 65.2 us -> 60 us
    pallas_call x1, Pallas kernels: 63 us -> 57.8 us  [local(): pl.pallas_call(functools.partial(kernel, outer_size, inner_size, groups,...]
where the time goes in v3:
time: 61 us; the launch traced here: 60.6 us
  Pallas kernels  60 us (98%)
  between operations  0.64 us (1%)
    pallas_call x1, Pallas kernels, local(): pl.pallas_call(functools.partial(kernel, outer_size, inner_size, groups,...  57.8 us
    pallas_call x1, Pallas kernels, local(): pl.pallas_call(copy_kernel, out_shape=(block, block, block), in_specs=[pl...  2.23 us

profile of v3, /device:TPU:0, one launch (start us, length us, event | category | flops | bytes accessed | tf_op | source)
XLA Modules:
  0.0 60.6 jit_solution(8446780149201618498)
XLA Ops:
  0.6 57.8 %shard_map.67 = (bf16[256,1024]{1,0:T(8,128)(2,1)}, bf16[256,1024]{1,0:T(8,128)(2,1)}, bf16[256,1024]{1,0:T(8,128)(2,1)}) custom-call(bf16[256,1024]{1,0:T(8,128)(2,1)} %q_hbm.1, bf16[256,1024]{1,0:T(8,128)(2,1)} %k_hbm.1, bf16[256,1024]{1,0:T(8,128)(2,1)} %v_hbm.1, bf16[256,1024]{1,0:T(8,128)(2,1)} %do_hbm.1), custom_call_target="tpu_custom_call" | custom-call | tf_op jit(solution)/shard_map/pallas_call | solution.py:323
  58.4 2.2 %shard_map.68 = (bf16[256,1024]{1,0:T(8,128)(2,1)}, bf16[256,1024]{1,0:T(8,128)(2,1)}, bf16[256,1024]{1,0:T(8,128)(2,1)}) custom-call(bf16[256,1024]{1,0:T(8,128)(2,1)} %get-tuple-element.6.refs_0_, bf16[256,1024]{1,0:T(8,128)(2,1)} %get-tuple-element.7.refs_1_, bf16[256,1024]{1,0:T(8,128)(2,1)} %get-tuple-element.8.refs_2_), custom_call_target="tpu_custom_call" | custom-call | tf_op jit(solution)/shard_map/pallas_call | solution.py:354

commit v4 on v3

--- a/solution.py
+++ b/solution.py
@@ -10,14 +10,14 @@
 HEAD = 64
 COLS = 128
 MESH = pl.DeviceIdType.MESH
-AHEAD = 2
+AHEAD = 3
 BATCHES = ((0,4),(4,2),(6,2))
 LAG_B = 6
 LAG_K = 7
 LAG_E = 8
 HOP_LEAD = 1
 NT = (((1,), (1,)), ((), ()))
-RELAYS = {2: (1, 3, 6), 4: (2, 4, 7)}
+RELAYS = {2: (1, 3, 5), 4: (2, 4, 6)}
 RELAYED = sum(RELAYS.values(), ())
 
 

time: 61 us -> 59.4 us (0.974)
  Pallas kernels: 60 us -> 58.6 us
    pallas_call x1, Pallas kernels: 57.8 us -> 56.3 us  [local(): pl.pallas_call(functools.partial(kernel, outer_size, inner_size, groups,...]
where the time goes in v4:
time: 59.4 us; the launch traced here: 59.2 us
  Pallas kernels  58.6 us (99%)
  between operations  0.64 us (1%)
    pallas_call x1, Pallas kernels, local(): pl.pallas_call(functools.partial(kernel, outer_size, inner_size, groups,...  56.3 us
    pallas_call x1, Pallas kernels, local(): pl.pallas_call(copy_kernel, out_shape=(block, block, block), in_specs=[pl...  2.23 us

profile of v4, /device:TPU:0, one launch (start us, length us, event | category | flops | bytes accessed | tf_op | source)
XLA Modules:
  0.0 59.2 jit_solution(1351473329531052230)
XLA Ops:
  0.6 56.3 %shard_map.67 = (bf16[256,1024]{1,0:T(8,128)(2,1)}, bf16[256,1024]{1,0:T(8,128)(2,1)}, bf16[256,1024]{1,0:T(8,128)(2,1)}) custom-call(bf16[256,1024]{1,0:T(8,128)(2,1)} %q_hbm.1, bf16[256,1024]{1,0:T(8,128)(2,1)} %k_hbm.1, bf16[256,1024]{1,0:T(8,128)(2,1)} %v_hbm.1, bf16[256,1024]{1,0:T(8,128)(2,1)} %do_hbm.1), custom_call_target="tpu_custom_call" | custom-call | tf_op jit(solution)/shard_map/pallas_call | solution.py:323
  57.0 2.2 %shard_map.68 = (bf16[256,1024]{1,0:T(8,128)(2,1)}, bf16[256,1024]{1,0:T(8,128)(2,1)}, bf16[256,1024]{1,0:T(8,128)(2,1)}) custom-call(bf16[256,1024]{1,0:T(8,128)(2,1)} %get-tuple-element.6.refs_0_, bf16[256,1024]{1,0:T(8,128)(2,1)} %get-tuple-element.7.refs_1_, bf16[256,1024]{1,0:T(8,128)(2,1)} %get-tuple-element.8.refs_2_), custom_call_target="tpu_custom_call" | custom-call | tf_op jit(solution)/shard_map/pallas_call | solution.py:354

commit v5 on v4

--- a/solution.py
+++ b/solution.py
@@ -27,6 +27,7 @@
     dq_out, dk_out, dv_out,
     qd, kv, km, vm, kt, e_all, dp_all, p_low, ds_low,
     part, stats, stats_in, dq_own, dq_send, dq_in, passing,
+    dq_held, dk_held, dv_held, store_sem,
     load_sem, qd_send, qd_recv, stats_send, stats_recv,
     dq_ssem, dq_rsem, hop_send, hop_recv, pass_send,
 ):
@@ -44,6 +45,12 @@
         src = (k_hbm, v_hbm)[which]
         return pltpu.make_async_copy(src.at[:, pl.ds(g * COLS, COLS)], kv.at[g, which], load_sem.at[2 + which, g])
 
+    def store(g, which):
+        src = (dq_held, dk_held, dv_held)[which]
+        dst = (dq_out, dk_out, dv_out)[which]
+        columns = pl.ds(pl.multiple_of(g * COLS, COLS), COLS)
+        return pltpu.make_async_copy(src.at[g], dst.at[:, columns], store_sem.at[which, g])
+
     def send_qd(g, r):
         return pltpu.make_async_remote_copy(
             qd.at[g, :, 0], qd.at[g, :, r + 1], qd_send.at[r, g], qd_recv.at[r, g],
@@ -87,6 +94,21 @@
             dq_send.at[g, r], dq_in.at[g, r], dq_ssem.at[r, g], dq_rsem.at[r, g],
             device_id=after[r], device_id_type=MESH)
 
+    barrier = pltpu.get_barrier_semaphore()
+    for device in before + after + across:
+        pl.semaphore_signal(barrier, inc=1, device_id=device, device_id_type=MESH)
+    peers = {n: 6 for n in range(half)}
+    for relay in RELAYS:
+        @pl.when(place == relay)
+        def _():
+            pl.semaphore_signal(barrier, inc=1, device_id=(other, i), device_id_type=MESH)
+
+        @pl.when(place == half - 1)
+        def _():
+            pl.semaphore_signal(barrier, inc=1, device_id=(base + relay, i), device_id_type=MESH)
+
+        peers[0] += 1
+        peers[relay] += 1
     for g in range(groups):
         for which in range(2):
             load_qd(g, which).start()
@@ -94,21 +116,6 @@
         for which in range(2):
             load_kv(g, which).start()
 
-    barrier = pltpu.get_barrier_semaphore()
-    for device in before + after + across:
-        pl.semaphore_signal(barrier, inc=1, device_id=device, device_id_type=MESH)
-    peers = {n: 6 for n in range(half)}
-    for relay in RELAYS:
-        @pl.when(place == relay)
-        def _():
-            pl.semaphore_signal(barrier, inc=1, device_id=(other, i), device_id_type=MESH)
-
-        @pl.when(place == half - 1)
-        def _():
-            pl.semaphore_signal(barrier, inc=1, device_id=(base + relay, i), device_id_type=MESH)
-
-        peers[0] += 1
-        peers[relay] += 1
     for count in sorted(set(peers.values())):
         @pl.when(functools.reduce(lambda a, b: a | b, [place == n for n in range(half) if peers[n] == count]))
         def _():
@@ -213,22 +220,27 @@
                 send_dq(g, r - 1).start()
 
     def key_gradients(g):
-        columns = pl.ds(pl.multiple_of(g * COLS, COLS), COLS)
         q = qd[g, 0].reshape(3 * rows, COLS)
         do = qd[g, 1].reshape(3 * rows, COLS)
         dv = [jnp.dot(p_low[g, h], do, preferred_element_type=jnp.float32) for h in range(2)]
-        dv_out[:, columns] = jnp.where(first, dv[0], dv[1]).astype(jnp.bfloat16)
+        dv_held[g] = jnp.where(first, dv[0], dv[1]).astype(jnp.bfloat16)
         dk = [jnp.dot(ds_low[g, h], q, preferred_element_type=jnp.float32) for h in range(2)]
-        dk_out[:, columns] = (jnp.where(first, dk[0], dk[1]) * scale).astype(jnp.bfloat16)
+        dk_held[g] = (jnp.where(first, dk[0], dk[1]) * scale).astype(jnp.bfloat16)
+        store(g, 1).start()
+        store(g, 2).start()
 
     def finish(g):
         for r in range(2):
             send_dq(g, r).wait_recv()
         dq = dq_own[g] + dq_in[g, 0].astype(jnp.float32) + dq_in[g, 1].astype(jnp.float32)
-        columns = pl.ds(pl.multiple_of(g * COLS, COLS), COLS)
-        dq_out[:, columns] = dq.T.astype(jnp.bfloat16)
+        dq_held[g] = dq.T.astype(jnp.bfloat16)
+        store(g, 0).start()
 
     def step(t, carry):
+        @pl.when(t < groups - AHEAD)
+        def _():
+            start_group(t + AHEAD)
+
         @pl.when(t < groups)
         def _():
             scores(t, 0)
@@ -252,10 +264,6 @@
             def _():
                 share(b)
 
-        @pl.when(t < groups - AHEAD)
-        def _():
-            start_group(t + AHEAD)
-
         @pl.when((t >= LAG_B) & (t < groups + LAG_B))
         def _():
             gradients(t - LAG_B)
@@ -275,6 +283,8 @@
     def drain(g, carry):
         for r in range(2):
             send_dq(g, r).wait_send()
+        for which in range(3):
+            store(g, which).wait()
         send_qd(g, 0).wait_send()
 
         @pl.when(jnp.logical_not(wraps & among(g, RELAYED)))
@@ -324,7 +334,7 @@
         functools.partial(kernel, outer_size, inner_size, groups, rows),
         out_shape=(block, block, block),
         in_specs=[pl.BlockSpec(memory_space=pl.ANY)] * 4,
-        out_specs=[pl.BlockSpec(memory_space=pltpu.VMEM)] * 3,
+        out_specs=[pl.BlockSpec(memory_space=pl.ANY)] * 3,
         scratch_shapes=[
             pltpu.VMEM((groups, 2, 3, rows, COLS), low),
             pltpu.VMEM((groups, 2, rows, COLS), low),
@@ -342,6 +352,10 @@
             pltpu.VMEM((groups, 2, COLS, rows), low),
             pltpu.VMEM((groups, 2, COLS, rows), low),
             pltpu.VMEM((3, 2, rows, COLS), low),
+            pltpu.VMEM((groups, rows, COLS), low),
+            pltpu.VMEM((groups, rows, COLS), low),
+            pltpu.VMEM((groups, rows, COLS), low),
+            dma((3, groups)),
             dma((4, groups)),
             dma((2, groups)), dma((2, groups)),
             dma((6, len(BATCHES))), dma((6, len(BATCHES))),

time: 59.4 us -> 58.9 us (level)
  no operation moved by 1% of the time
where the time goes in v5:
time: 58.9 us; the launch traced here: 58.7 us
  Pallas kernels  58.1 us (99%)
  between operations  0.64 us (1%)
    pallas_call x1, Pallas kernels, local(): pl.pallas_call(functools.partial(kernel, outer_size, inner_size, groups,...  55.9 us
    pallas_call x1, Pallas kernels, local(): pl.pallas_call(copy_kernel, out_shape=(block, block, block), in_specs=[pl...  2.23 us

profile of v5, /device:TPU:0, one launch (start us, length us, event | category | flops | bytes accessed | tf_op | source)
XLA Modules:
  0.0 58.7 jit_solution(4200362876513765214)
XLA Ops:
  0.6 55.9 %shard_map.67 = (bf16[256,1024]{1,0:T(8,128)(2,1)}, bf16[256,1024]{1,0:T(8,128)(2,1)}, bf16[256,1024]{1,0:T(8,128)(2,1)}) custom-call(bf16[256,1024]{1,0:T(8,128)(2,1)} %q_hbm.1, bf16[256,1024]{1,0:T(8,128)(2,1)} %k_hbm.1, bf16[256,1024]{1,0:T(8,128)(2,1)} %v_hbm.1, bf16[256,1024]{1,0:T(8,128)(2,1)} %do_hbm.1), custom_call_target="tpu_custom_call" | custom-call | tf_op jit(solution)/shard_map/pallas_call | solution.py:333
  56.5 2.2 %shard_map.68 = (bf16[256,1024]{1,0:T(8,128)(2,1)}, bf16[256,1024]{1,0:T(8,128)(2,1)}, bf16[256,1024]{1,0:T(8,128)(2,1)}) custom-call(bf16[256,1024]{1,0:T(8,128)(2,1)} %get-tuple-element.6.refs_0_, bf16[256,1024]{1,0:T(8,128)(2,1)} %get-tuple-element.7.refs_1_, bf16[256,1024]{1,0:T(8,128)(2,1)} %get-tuple-element.8.refs_2_), custom_call_target="tpu_custom_call" | custom-call | tf_op jit(solution)/shard_map/pallas_call | solution.py:368

commit v6 on v5

--- a/solution.py
+++ b/solution.py
@@ -10,8 +10,8 @@
 HEAD = 64
 COLS = 128
 MESH = pl.DeviceIdType.MESH
-AHEAD = 3
-BATCHES = ((0,4),(4,2),(6,2))
+AHEAD = 4
+BATCHES = ((0,2),(2,2),(4,2),(6,2))
 LAG_B = 6
 LAG_K = 7
 LAG_E = 8

time: 58.9 us -> 58.8 us (level)
  no operation moved by 1% of the time
where the time goes in v6:
time: 58.8 us; the launch traced here: 58.6 us
  Pallas kernels  58 us (99%)
  between operations  0.64 us (1%)
    pallas_call x1, Pallas kernels, local(): pl.pallas_call(functools.partial(kernel, outer_size, inner_size, groups,...  55.8 us
    pallas_call x1, Pallas kernels, local(): pl.pallas_call(copy_kernel, out_shape=(block, block, block), in_specs=[pl...  2.23 us

profile of v6, /device:TPU:0, one launch (start us, length us, event | category | flops | bytes accessed | tf_op | source)
XLA Modules:
  0.0 58.6 jit_solution(10340459417639549503)
XLA Ops:
  0.6 55.8 %shard_map.67 = (bf16[256,1024]{1,0:T(8,128)(2,1)}, bf16[256,1024]{1,0:T(8,128)(2,1)}, bf16[256,1024]{1,0:T(8,128)(2,1)}) custom-call(bf16[256,1024]{1,0:T(8,128)(2,1)} %q_hbm.1, bf16[256,1024]{1,0:T(8,128)(2,1)} %k_hbm.1, bf16[256,1024]{1,0:T(8,128)(2,1)} %v_hbm.1, bf16[256,1024]{1,0:T(8,128)(2,1)} %do_hbm.1), custom_call_target="tpu_custom_call" | custom-call | tf_op jit(solution)/shard_map/pallas_call | solution.py:333
  56.4 2.2 %shard_map.68 = (bf16[256,1024]{1,0:T(8,128)(2,1)}, bf16[256,1024]{1,0:T(8,128)(2,1)}, bf16[256,1024]{1,0:T(8,128)(2,1)}) custom-call(bf16[256,1024]{1,0:T(8,128)(2,1)} %get-tuple-element.6.refs_0_, bf16[256,1024]{1,0:T(8,128)(2,1)} %get-tuple-element.7.refs_1_, bf16[256,1024]{1,0:T(8,128)(2,1)} %get-tuple-element.8.refs_2_), custom_call_target="tpu_custom_call" | custom-call | tf_op jit(solution)/shard_map/pallas_call | solution.py:368
